TPU v7x, 32 devices: a whole 2x2x4 slice. The times are simulated.
32 devices in a mesh: dp: 16 (over z, x, core), tensor: 2 (over y).
Axes of the slice: x: 2, y: 2, z: 4, core: 2. Of those that a mesh axis runs over, the one named last changes fastest.
Arguments:
- tokens: bfloat16 [32768, 768], P(('dp', 'tensor')), may hold values from -6 to 6
- teacher: bfloat16 [32768, 768], P(('dp', 'tensor')), may hold values from -23 to 23
- segments: int32 [64, 512], P(('dp', 'tensor')), may hold values from 0 to 3, never falling along the last dimension, each value on 1 to 256 neighbouring positions
- qkv_weight: bfloat16 [768, 3, 768], P('dp', None, 'tensor'), may hold values from -0.21875 to 0.21875
- qkv_bias: float32 [2, 768], replicated, may hold values from -3 to 3
- out_weight: bfloat16 [768, 768], P('dp', 'tensor'), may hold values from -1.75 to 1.75
- out_bias: float32 [768], replicated, may hold values from -3 to 3
- up_weight: bfloat16 [768, 3072], P('dp', 'tensor'), may hold values from -0.21875 to 0.21875
- up_bias: float32 [3072], replicated, may hold values from -3 to 3
- down_weight: bfloat16 [768, 3072], P('dp', 'tensor'), may hold values from -0.21875 to 0.21875
- down_bias: float32 [768], replicated, may hold values from -3 to 3
- first_gain: float32 [768], replicated, may hold values from 0.5 to 1.5
- first_shift: float32 [768], replicated, may hold values from -2 to 2
- second_gain: float32 [768], replicated, may hold values from 0.5 to 1.5
- second_shift: float32 [768], replicated, may hold values from -2 to 2
- head_logit: float32 [12], replicated, may hold values from -1 to 3
- unit_logit: float32 [3072], replicated, may hold values from -1 to 3
- width_logit: float32 [768], replicated, may hold values from -1 to 3
- layer_logit: float32 [2], replicated, may hold values from -1 to 3
- head_noise: float32 [12], replicated, may hold values from 0.05 to 0.95
- unit_noise: float32 [3072], replicated, may hold values from 0.05 to 0.95
- width_noise: float32 [768], replicated, may hold values from 0.05 to 0.95
- layer_noise: float32 [2], replicated, may hold values from 0.05 to 0.95
Outputs:
- activations: bfloat16 [32768, 768], P(('dp', 'tensor'))
- distill_loss: float32 [], replicated
- tokens_grad: float32 [32768, 768], P(('dp', 'tensor'))
- qkv_weight_grad: float32 [768, 3, 768], P('dp', None, 'tensor')
- qkv_bias_grad: float32 [2, 768], replicated
- out_weight_grad: float32 [768, 768], P('dp', 'tensor')
- out_bias_grad: float32 [768], replicated
- up_weight_grad: float32 [768, 3072], P('dp', 'tensor')
- up_bias_grad: float32 [3072], replicated
- down_weight_grad: float32 [768, 3072], P('dp', 'tensor')
- down_bias_grad: float32 [768], replicated
- first_gain_grad: float32 [768], replicated
- first_shift_grad: float32 [768], replicated
- second_gain_grad: float32 [768], replicated
- second_shift_grad: float32 [768], replicated
- head_logit_grad: float32 [12], replicated
- unit_logit_grad: float32 [3072], replicated
- width_logit_grad: float32 [768], replicated
- layer_logit_grad: float32 [2], replicated
Inputs may be any that keep to these rules, and one draw needn't show every extreme that they name: `segments`: each row is one sequence; its item ids never fall along the row, every id occurs in every row, and an item spans at most 256 rows.
All inputs are finite; a program needn't handle non-finite values.
Results may differ from a plain program's by a relative error of at most 0.012.
The roundings to bfloat16 on the way count: a program that leaves them out, or rounds other values in their place, can miss the bound.
Values may be sent and summed in bfloat16 or wider, within the bound.
A program may use at most 192 MiB of HBM per device.

v0:
```python
import jax
import jax.numpy as jnp
from jax import lax
from jax.sharding import PartitionSpec as P

D = 768
HEADS = 12
HEAD_DIM = 64
FF = 3072
SEQ_LEN = 512
MICRO = 2
SEQ_MB = 1


BETA = 2.0 / 3.0
EPS = 1e-12
NEG = -1e30
ROWS_DIMS = (((0,), (0,)), ((), ()))
COLS_DIMS = (((1,), (1,)), ((), ()))


def gate_values(noise, logit):
    return jax.nn.sigmoid((jnp.log(noise) - jnp.log1p(-noise) + logit) / BETA)


def layer_norm(value, gain, shift):
    mean = jnp.mean(value, axis=-1, keepdims=True)
    centred = value - mean
    var = jnp.mean(centred * centred, axis=-1, keepdims=True)
    return centred * lax.rsqrt(var + EPS) * gain + shift


def matmul(left, right, dims):
    return lax.dot_general(left, right, dims, preferred_element_type=jnp.float32)


def head_shape(array, marks):
    return array.reshape(marks.shape[0], SEQ_LEN, array.shape[1] // HEAD_DIM, HEAD_DIM)


def masked_scores(query, keys, marks):
    scores = jnp.einsum("qhd,khd->hqk", query, keys, preferred_element_type=jnp.float32)
    return jnp.where((marks[:, None] == marks[None, :])[None], scores, NEG)


def forward_attention(query, keys, values, marks):

    def forward_single(item):
        seq_query, seq_keys, seq_values, seq_marks = item
        scores = masked_scores(seq_query, seq_keys, seq_marks)
        top = jnp.max(scores, axis=-1, keepdims=True)
        expo = jnp.exp(scores - top)
        total = jnp.sum(expo, axis=-1, keepdims=True)
        probs = (expo / total).astype(jnp.bfloat16)
        context = jnp.einsum("hqk,khd->qhd", probs, seq_values, preferred_element_type=jnp.float32)
        return (context.astype(jnp.bfloat16), (top + jnp.log(total))[..., 0])

    context, logsum = lax.map(
        forward_single,
        (head_shape(query, marks), head_shape(keys, marks), head_shape(values, marks), marks),
    )
    return (context.reshape(query.shape), logsum)


def backward_attention(query, keys, values, marks, logsum, grad_context):

    def backward_single(item):
        seq_query, seq_keys, seq_values, seq_marks, seq_logsum, seq_grad = item
        scores = masked_scores(seq_query, seq_keys, seq_marks)
        probs = jnp.exp(scores - seq_logsum[..., None])
        grad_probs = jnp.einsum(
            "qhd,khd->hqk", seq_grad, seq_values, preferred_element_type=jnp.float32
        )
        delta = jnp.sum(grad_probs * probs, axis=-1, keepdims=True)
        grad_scores = (probs * (grad_probs - delta)).astype(jnp.bfloat16)
        grad_query = jnp.einsum(
            "hqk,khd->qhd", grad_scores, seq_keys, preferred_element_type=jnp.float32
        )
        grad_keys = jnp.einsum(
            "hqk,qhd->khd", grad_scores, seq_query, preferred_element_type=jnp.float32
        )
        grad_values = jnp.einsum(
            "hqk,qhd->khd", probs.astype(jnp.bfloat16), seq_grad, preferred_element_type=jnp.float32
        )
        return (grad_query, grad_keys, grad_values)

    grad_query, grad_keys, grad_values = lax.map(
        backward_single,
        (
            head_shape(query, marks),
            head_shape(keys, marks),
            head_shape(values, marks),
            marks,
            logsum,
            head_shape(grad_context, marks),
        ),
    )
    return (
        grad_query.reshape(query.shape),
        grad_keys.reshape(query.shape),
        grad_values.reshape(query.shape),
    )


def body(
    tokens,
    teacher,
    segments,
    qkv_weight,
    qkv_bias,
    out_weight,
    out_bias,
    up_weight,
    up_bias,
    down_weight,
    down_bias,
    first_gain,
    first_shift,
    second_gain,
    second_shift,
    head_logit,
    unit_logit,
    width_logit,
    layer_logit,
    head_noise,
    unit_noise,
    width_noise,
    layer_noise,
):
    width = tokens.shape[1]
    rows = SEQ_MB * SEQ_LEN
    scale = HEAD_DIM ** (-0.5)
    local = qkv_weight.shape[2]
    units = up_weight.shape[1]
    col_start = lax.axis_index("tensor") * local
    unit_start = lax.axis_index("tensor") * units
    head_start = col_start // HEAD_DIM
    head_count = local // HEAD_DIM
    head_noise_own = lax.dynamic_slice_in_dim(head_noise, head_start, head_count, 0)
    head_logit_own = lax.dynamic_slice_in_dim(head_logit, head_start, head_count, 0)
    unit_noise_own = lax.dynamic_slice_in_dim(unit_noise, unit_start, units, 0)
    unit_logit_own = lax.dynamic_slice_in_dim(unit_logit, unit_start, units, 0)
    qkv_bias_own = lax.dynamic_slice_in_dim(qkv_bias, col_start, local, 1)
    up_bias_own = lax.dynamic_slice_in_dim(up_bias, unit_start, units, 0)
    head_gate = gate_values(head_noise_own, head_logit_own)
    head_cols = jnp.repeat(head_gate, HEAD_DIM)

    def first_piece(resid, attn, bias, wlogit, llogit, gain, shift):
        width_gate = gate_values(width_noise, wlogit)
        layer_gate = gate_values(layer_noise, llogit)
        return layer_norm(resid + (attn + bias) * (layer_gate[0] * width_gate), gain, shift)

    def second_piece(normed, ffn, bias, wlogit, llogit, gain, shift):
        width_gate = gate_values(width_noise, wlogit)
        layer_gate = gate_values(layer_noise, llogit)
        return layer_norm(normed + (ffn + bias) * (layer_gate[1] * width_gate), gain, shift)

    def unit_piece(pre, ulogit):
        return jax.nn.gelu(pre, approximate=False) * gate_values(unit_noise_own, ulogit)

    shards = (qkv_weight, out_weight, up_weight, down_weight)
    f32 = jnp.float32
    sum_qkv = jnp.zeros((width, 3 * local), f32)
    sum_out = jnp.zeros((width, local), f32)
    sum_up = jnp.zeros((width, units), f32)
    sum_down = jnp.zeros((width, units), f32)
    sum_qkv_bias = jnp.zeros((2, local), f32)
    sum_up_bias = jnp.zeros((units,), f32)
    sum_head = jnp.zeros((head_count,), f32)
    sum_unit_logit = jnp.zeros((units,), f32)
    sum_out_bias = jnp.zeros((width,), f32)
    sum_down_bias = jnp.zeros((width,), f32)
    sum_first_gain = jnp.zeros((width,), f32)
    sum_first_shift = jnp.zeros((width,), f32)
    sum_second_gain = jnp.zeros((width,), f32)
    sum_second_shift = jnp.zeros((width,), f32)
    sum_width_logit = jnp.zeros((width,), f32)
    sum_layer_logit = jnp.zeros((2,), f32)
    loss_sum = jnp.zeros((), f32)
    results = []
    token_grads = []
    for micro in range(MICRO):
        own = tokens[micro * rows : (micro + 1) * rows]
        own_marks = segments[micro * SEQ_MB : (micro + 1) * SEQ_MB]
        micro_weights = (
            lax.all_gather(shards[0], "dp", axis=0, tiled=True),
            lax.all_gather(shards[1], "dp", axis=0, tiled=True),
            lax.all_gather(shards[2], "dp", axis=0, tiled=True),
            lax.all_gather(shards[3], "dp", axis=0, tiled=True),
        )
        qkv_full, out_full, up_full, down_full = micro_weights
        qkv_flat = qkv_full.reshape(width, 3 * local)
        gathered, marks = (
            lax.all_gather(own, "tensor", axis=0, tiled=True),
            lax.all_gather(own_marks, "tensor", axis=0, tiled=True),
        )
        mixed = jnp.dot(gathered, qkv_flat, preferred_element_type=f32)
        query = ((mixed[:, :local] + qkv_bias_own[0]) * scale).astype(jnp.bfloat16)
        keys = mixed[:, local : 2 * local].astype(jnp.bfloat16)
        value_pre = mixed[:, 2 * local :] + qkv_bias_own[1]
        values = (value_pre * head_cols).astype(jnp.bfloat16)
        context, logsum = forward_attention(query, keys, values, marks)
        attn = lax.psum_scatter(
            matmul(context, out_full, COLS_DIMS), "tensor", scatter_dimension=0, tiled=True
        )
        normed, first_back = jax.vjp(
            first_piece,
            own.astype(f32),
            attn,
            out_bias,
            width_logit,
            layer_logit,
            first_gain,
            first_shift,
        )
        normed_low = normed.astype(jnp.bfloat16)
        spread = lax.all_gather(normed_low, "tensor", axis=0, tiled=True)
        pre_up = jnp.dot(spread, up_full, preferred_element_type=f32) + up_bias_own
        activ, unit_back = jax.vjp(unit_piece, pre_up, unit_logit_own)
        activ_low = activ.astype(jnp.bfloat16)
        ffn = lax.psum_scatter(
            matmul(activ_low, down_full, COLS_DIMS), "tensor", scatter_dimension=0, tiled=True
        )
        result, second_back = jax.vjp(
            second_piece,
            normed,
            ffn,
            down_bias,
            width_logit,
            layer_logit,
            second_gain,
            second_shift,
        )
        diff = result - teacher[micro * rows : (micro + 1) * rows].astype(f32)
        loss_sum = loss_sum + 0.5 * jnp.sum(diff * diff)
        results.append(result.astype(jnp.bfloat16))
        g_resid2, g_ffn, g_down_bias, g_width2, g_layer2, g_gain2, g_shift2 = second_back(diff)
        g_ffn_low = g_ffn.astype(jnp.bfloat16)
        g_ffn_all = lax.all_gather(g_ffn_low, "tensor", axis=0, tiled=True)
        g_activ = jnp.dot(g_ffn_all, down_full, preferred_element_type=f32)
        sum_down = sum_down + matmul(g_ffn_all, activ_low, ROWS_DIMS)
        g_pre, g_unit = unit_back(g_activ)
        g_pre_low = g_pre.astype(jnp.bfloat16)
        sum_up_bias = sum_up_bias + jnp.sum(g_pre_low, axis=0, dtype=f32)
        sum_up = sum_up + matmul(spread, g_pre_low, ROWS_DIMS)
        sum_unit_logit = sum_unit_logit + g_unit
        g_hidden = lax.psum_scatter(
            matmul(g_pre_low, up_full, COLS_DIMS), "tensor", scatter_dimension=0, tiled=True
        )
        g_normed = g_resid2 + g_hidden
        g_resid1, g_attn, g_out_bias, g_width1, g_layer1, g_gain1, g_shift1 = first_back(g_normed)
        g_attn_low = g_attn.astype(jnp.bfloat16)
        g_attn_all = lax.all_gather(g_attn_low, "tensor", axis=0, tiled=True)
        g_context = jnp.dot(g_attn_all, out_full, preferred_element_type=f32).astype(jnp.bfloat16)
        sum_out = sum_out + matmul(g_attn_all, context, ROWS_DIMS)
        g_query, g_keys, g_values = backward_attention(
            query, keys, values, marks, logsum, g_context
        )
        g_query_low = (g_query * scale).astype(jnp.bfloat16)
        g_values_low = (g_values * head_cols).astype(jnp.bfloat16)
        g_head_cols = jnp.sum(g_values * value_pre, axis=0)
        sum_head = sum_head + jnp.sum(g_head_cols.reshape(-1, HEAD_DIM), axis=1)
        g_mix = jnp.concatenate([g_query_low, g_keys.astype(jnp.bfloat16), g_values_low], axis=1)
        sum_qkv = sum_qkv + matmul(gathered, g_mix, ROWS_DIMS)
        sum_qkv_bias = sum_qkv_bias + jnp.stack(
            [jnp.sum(g_query_low, axis=0, dtype=f32), jnp.sum(g_values_low, axis=0, dtype=f32)]
        )
        g_input = lax.psum_scatter(
            matmul(g_mix, qkv_flat, COLS_DIMS).astype(jnp.bfloat16),
            "tensor",
            scatter_dimension=0,
            tiled=True,
        ).astype(jnp.float32)
        token_grads.append(g_resid1 + g_input)
        sum_out_bias = sum_out_bias + g_out_bias
        sum_down_bias = sum_down_bias + g_down_bias
        sum_first_gain = sum_first_gain + g_gain1
        sum_first_shift = sum_first_shift + g_shift1
        sum_second_gain = sum_second_gain + g_gain2
        sum_second_shift = sum_second_shift + g_shift2
        sum_width_logit = sum_width_logit + g_width1 + g_width2
        sum_layer_logit = sum_layer_logit + g_layer1 + g_layer2
    _, head_back = jax.vjp(lambda logit: gate_values(head_noise_own, logit), head_logit_own)
    head_logit_local = head_back(sum_head)[0]
    big_sums = (sum_qkv.reshape(width, 3, local), sum_out, sum_up, sum_down)
    qkv_grad, out_grad, up_grad, down_grad = (
        lax.psum_scatter(big_sums[0], "dp", scatter_dimension=0, tiled=True),
        lax.psum_scatter(big_sums[1], "dp", scatter_dimension=0, tiled=True),
        lax.psum_scatter(big_sums[2], "dp", scatter_dimension=0, tiled=True),
        lax.psum_scatter(big_sums[3], "dp", scatter_dimension=0, tiled=True),
    )
    qkv_bias_place = lax.dynamic_update_slice_in_dim(
        jnp.zeros((2, D), f32), sum_qkv_bias, col_start, 1
    )
    up_bias_place = lax.dynamic_update_slice_in_dim(
        jnp.zeros((FF,), f32), sum_up_bias, unit_start, 0
    )
    head_place = lax.dynamic_update_slice_in_dim(
        jnp.zeros((HEADS,), f32), head_logit_local, head_start, 0
    )
    unit_place = lax.dynamic_update_slice_in_dim(
        jnp.zeros((FF,), f32), sum_unit_logit, unit_start, 0
    )
    (
        qkv_bias_grad,
        up_bias_grad,
        head_grad,
        unit_grad,
        out_bias_grad,
        down_bias_grad,
        first_gain_grad,
        first_shift_grad,
        second_gain_grad,
        second_shift_grad,
        width_grad,
        layer_grad,
        loss_total,
    ) = lax.psum(
        (
            qkv_bias_place,
            up_bias_place,
            head_place,
            unit_place,
            sum_out_bias,
            sum_down_bias,
            sum_first_gain,
            sum_first_shift,
            sum_second_gain,
            sum_second_shift,
            sum_width_logit,
            sum_layer_logit,
            loss_sum,
        ),
        ("dp", "tensor"),
    )
    all_tokens = rows * MICRO * lax.axis_size("dp") * lax.axis_size("tensor")
    return (
        jnp.concatenate(results, axis=0),
        loss_total / all_tokens,
        jnp.concatenate(token_grads, axis=0),
        qkv_grad,
        qkv_bias_grad,
        out_grad,
        out_bias_grad,
        up_grad,
        up_bias_grad,
        down_grad,
        down_bias_grad,
        first_gain_grad,
        first_shift_grad,
        second_gain_grad,
        second_shift_grad,
        head_grad,
        unit_grad,
        width_grad,
        layer_grad,
    )


def solution(mesh):
    in_specs = (
        P(("dp", "tensor"), None),
        P(("dp", "tensor"), None),
        P(("dp", "tensor"), None),
        P("dp", None, "tensor"),
        P(),
        P("dp", "tensor"),
        P(),
        P("dp", "tensor"),
        P(),
        P("dp", "tensor"),
        P(),
        P(),
        P(),
        P(),
        P(),
        P(),
        P(),
        P(),
        P(),
        P(),
        P(),
        P(),
        P(),
    )
    out_specs = (
        P(("dp", "tensor"), None),
        P(),
        P(("dp", "tensor"), None),
        P("dp", None, "tensor"),
        P(),
        P("dp", "tensor"),
        P(),
        P("dp", "tensor"),
        P(),
        P("dp", "tensor"),
        P(),
        P(),
        P(),
        P(),
        P(),
        P(),
        P(),
        P(),
        P(),
    )
    return jax.shard_map(body, mesh=mesh, in_specs=in_specs, out_specs=out_specs, check_vma=False)
```

profile of v0, /device:TPU:0, one launch (start us, length us, event | category | flops | bytes accessed | tf_op | source)
XLA Modules:
  0.0 1140.9 jit_solution(17623954100167082474)
XLA Ops:
  17.6 24.6 %all_gather.49 = bf16[768,384]{1,0:T(8,128)(2,1)S(1)} all-gather(bf16[48,384]{1,0:T(8,128)(2,1)S(1)} %copy-done.77), channel_id=1, replica_groups=mesh['dp'=16,'tensor'=2] {'dp'}, dimensions={0}, use_global_device_ids=true | all-gather | bytes 626688 | tf_op jit(solution)/shard_map/all_gather | solution.py:187
  42.3 12.3 %all-gather.16.cloned.1.call-done = bf16[768,3,384]{2,0,1:T(8,128)(2,1)} async-done(((bf16[48,3,384]{2,0,1:T(8,128)(2,1)}), bf16[768,3,384]{2,0,1:T(8,128)(2,1)}) %all-gather.16.cloned.1.call-update) | async-done | bytes 1769488 | tf_op jit(solution)/shard_map/all_gather | solution.py:186
  57.2 25.6 %all-gather.24.cloned.1.call-done = bf16[1024,768]{1,0:T(8,128)(2,1)} async-done(((bf16[512,768]{1,0:T(8,128)(2,1)}), bf16[1024,768]{1,0:T(8,128)(2,1)}) %all-gather.24.cloned.1.call-update) | async-done | bytes 1572880 | tf_op jit(solution)/shard_map/all_gather | solution.py:194
  89.6 22.6 %all-gather.14.cloned.1.call-done = bf16[1024,768]{1,0:T(8,128)(2,1)} async-done(((bf16[512,768]{1,0:T(8,128)(2,1)}), bf16[1024,768]{1,0:T(8,128)(2,1)}) %all-gather.14.cloned.1.call-update) | async-done | bytes 1572880 | tf_op jit(solution)/shard_map/all_gather | solution.py:194
  192.4 46.1 %reduce-scatter.13.cloned.1.call-done = f32[512,768]{1,0:T(8,128)} async-done(((f32[1024,768]{1,0:T(8,128)}), f32[512,768]{1,0:T(8,128)}) %reduce-scatter.13.cloned.1.call-update) | async-done | bytes 1572880 | tf_op jit(solution)/shard_map/reduce_scatter | solution.py:203
  246.3 36.7 %all-gather.20.cloned.1.call-done = bf16[768,1536]{1,0:T(8,128)(2,1)} async-done(((bf16[48,1536]{1,0:T(8,128)(2,1)}), bf16[768,1536]{1,0:T(8,128)(2,1)}) %all-gather.20.cloned.1.call-update) | async-done | bytes 2359312 | tf_op jit(solution)/shard_map/all_gather | solution.py:188
  283.0 28.1 %all-gather.26.cloned.1.call-done = bf16[1024,768]{1,0:T(8,128)(2,1)} async-done(((bf16[512,768]{1,0:T(8,128)(2,1)}), bf16[1024,768]{1,0:T(8,128)(2,1)}) %all-gather.26.cloned.1.call-update) | async-done | bytes 1572880 | tf_op jit(solution)/shard_map/all_gather | solution.py:217
  318.6 22.0 %all-gather.18.cloned.1.call-done = bf16[1024,768]{1,0:T(8,128)(2,1)} async-done(((bf16[512,768]{1,0:T(8,128)(2,1)}), bf16[1024,768]{1,0:T(8,128)(2,1)}) %all-gather.18.cloned.1.call-update) | async-done | bytes 1572880 | tf_op jit(solution)/shard_map/all_gather | solution.py:217
  340.5 33.4 %multiply_convert_fusion.3 = (bf16[1024,1536]{1,0:T(8,128)(2,1)}, f32[1024,1536]{1,0:T(8,128)}, bf16[1024,1536]{1,0:T(8,128)(2,1)}, f32[1024,1536]{1,0:T(8,128)}, f32[1024,1536]{1,0:T(8,128)}) fusion(f32[1536]{0:T(1024)S(1)} %add_divide_fusion, f32[1536]{0:T(1024)S(1)} %dynamic_slice.84, f32[1024,1536]{1,0:T(8,128)} %fusion.160, ...), kind=kOutput, calls=%fused_computation.143 | convolution fusion | flops 2626682880 | bytes 35401728 | tf_op jit(solution)/shard_map/dot_general | solution.py:218
  399.6 34.8 %reduce-scatter.15.cloned.1.call-done = f32[512,768]{1,0:T(8,128)} async-done(((f32[1024,768]{1,0:T(8,128)}), f32[512,768]{1,0:T(8,128)}) %reduce-scatter.15.cloned.1.call-update) | async-done | bytes 1572880 | tf_op jit(solution)/shard_map/reduce_scatter | solution.py:221
  434.4 45.7 %reduce-scatter.19.cloned.1.call-done = f32[512,768]{1,0:T(8,128)} async-done(((f32[1024,768]{1,0:T(8,128)}), f32[512,768]{1,0:T(8,128)}) %reduce-scatter.19.cloned.1.call-update) | async-done | bytes 1572880 | tf_op jit(solution)/shard_map/reduce_scatter | solution.py:221
  494.5 26.6 %all-gather.28.cloned.1.call-done = bf16[1024,768]{1,0:T(8,128)(2,1)} async-done(((bf16[512,768]{1,0:T(8,128)(2,1)}), bf16[1024,768]{1,0:T(8,128)(2,1)}) %all-gather.28.cloned.1.call-update) | async-done | bytes 1572880 | tf_op jit(solution)/shard_map/all_gather | solution.py:239
  528.5 21.4 %all-gather.32.cloned.1.call-done = bf16[1024,768]{1,0:T(8,128)(2,1)} async-done(((bf16[512,768]{1,0:T(8,128)(2,1)}), bf16[1024,768]{1,0:T(8,128)(2,1)}) %all-gather.32.cloned.1.call-update) | async-done | bytes 1572880 | tf_op jit(solution)/shard_map/all_gather | solution.py:239
  549.8 19.2 %multiply_reduce_fusion.2 = (f32[1536]{0:T(1024)}, f32[1536]{0:T(1024)}, f32[1536]{0:T(1024)}, bf16[1024,1536]{1,0:T(8,128)(2,1)}, f32[1536]{0:T(1024)}, /*index=5*/bf16[1024,1536]{1,0:T(8,128)(2,1)S(1)}) fusion(f32[1024,1536]{1,0:T(8,128)} %get-tuple-element.541, f32[1024,1536]{1,0:T(8,128)} %fusion.160, f32[1536]{0:T(1024)S(1)} %dynamic_slice.84, ...), kind=kOutput, calls=%fused_computation.124 | convolution fusion | flops 2481973248 | bytes 41717760 | tf_op jit(solution)/shard_map/dot_general | solution.py:240
  582.4 36.1 %reduce-scatter.25.cloned.1.call-done = f32[512,768]{1,0:T(8,128)} async-done(((f32[1024,768]{1,0:T(8,128)}), f32[512,768]{1,0:T(8,128)}) %reduce-scatter.25.cloned.1.call-update) | async-done | bytes 1572880 | tf_op jit(solution)/shard_map/reduce_scatter | solution.py:247
  618.5 45.6 %reduce-scatter.21.cloned.1.call-done = f32[512,768]{1,0:T(8,128)} async-done(((f32[1024,768]{1,0:T(8,128)}), f32[512,768]{1,0:T(8,128)}) %reduce-scatter.21.cloned.1.call-update) | async-done | bytes 1572880 | tf_op jit(solution)/shard_map/reduce_scatter | solution.py:247
  674.7 25.4 %all-gather.30.cloned.1.call-done = bf16[1024,768]{1,0:T(8,128)(2,1)} async-done(((bf16[512,768]{1,0:T(8,128)(2,1)}), bf16[1024,768]{1,0:T(8,128)(2,1)}) %all-gather.30.cloned.1.call-update) | async-done | bytes 1572880 | tf_op jit(solution)/shard_map/all_gather | solution.py:253
  707.1 23.0 %while.54 = (s32[]{:T(128)}, f32[2,512,6,64]{1,3,2,0:T(8,128)}, bf16[2,512,6,64]{1,3,2,0:T(8,128)(2,1)}, f32[2,512,6,64]{1,3,2,0:T(8,128)}, bf16[2,512,6,64]{1,3...) while((s32[]{:T(128)}, f32[2,512,6,64]{1,3,2,0:T(8,128)}, ...), condition=%wide.region_30.31_spmd, body=%wide.region_28.30_spmd.sunk | while | flops 1025766400 | bytes 69180672 | solution.py:87
  741.8 23.4 %while.55 = (s32[]{:T(128)}, f32[2,512,6,64]{1,3,2,0:T(8,128)}, bf16[2,512,6,64]{1,3,2,0:T(8,128)(2,1)}, f32[2,512,6,64]{1,3,2,0:T(8,128)}, bf16[2,512,6,64]{1,3...) while((s32[]{:T(128)}, f32[2,512,6,64]{1,3,2,0:T(8,128)}, ...), condition=%wide.region_39.40_spmd, body=%wide.region_37.39_spmd.sunk | while | flops 1025766400 | bytes 69180672 | solution.py:87
  843.6 41.5 %all-reduce.4 = (f32[]{:T(128)}, f32[2,768]{1,0:T(2,128)}, f32[768]{0:T(1024)}, f32[3072]{0:T(1024)}, f32[768]{0:T(1024)}, /*index=5*/f32[768]{0:T(1024)}, f32[7...) all-reduce(f32[]{:T(128)S(6)} %add.432, ...), channel_id=1, replica_groups=mesh['dp'=16,'tensor'=2] {'dp','tensor'}, use_global_device_ids=true, to_apply=%region_22.23 | all-reduce | flops 13071 | bytes 104568 | tf_op jit(solution)/shard_map/psum | solution.py:318
  891.9 28.7 %reduce-scatter.35.cloned.1.call-done = f32[48,1536]{1,0:T(8,128)} async-done(((f32[768,1536]{1,0:T(8,128)}), f32[48,1536]{1,0:T(8,128)}) %reduce-scatter.35.cloned.1.call-update) | async-done | bytes 294928 | tf_op jit(solution)/shard_map/reduce_scatter | solution.py:290
  920.6 79.6 %reduce-scatter.33.cloned.1.call-done = f32[48,1536]{1,0:T(8,128)} async-done(((f32[768,1536]{1,0:T(8,128)}), f32[48,1536]{1,0:T(8,128)}) %reduce-scatter.33.cloned.1.call-update) | async-done | bytes 294928 | tf_op jit(solution)/shard_map/reduce_scatter | solution.py:289
  1000.1 61.3 %reduce-scatter.31.cloned.1.call-done = f32[48,384]{1,0:T(8,128)} async-done(((f32[768,384]{1,0:T(8,128)}), f32[48,384]{1,0:T(8,128)}) %reduce-scatter.31.cloned.1.call-update) | async-done | bytes 73744 | tf_op jit(solution)/shard_map/reduce_scatter | solution.py:288
  1061.5 71.5 %reduce-scatter.29.cloned.1.call-done = f32[48,3,384]{2,0,1:T(8,128)} async-done(((f32[768,3,384]{2,0,1:T(8,128)}), f32[48,3,384]{2,0,1:T(8,128)}) %reduce-scatter.29.cloned.1.call-update) | async-done | bytes 221200 | tf_op jit(solution)/shard_map/reduce_scatter | solution.py:287
  (576 shorter events, 352.2 us)
Async XLA Ops:
  7.2 47.3 %all-gather.16.cloned.1.call-start = ((), (), s32[]{:S(2)}) async-start(), calls=%async_computation.13 | async-start | bytes 1880064 | tf_op jit(solution)/shard_map/all_gather | solution.py:186
  8.0 74.8 %all-gather.24.cloned.1.call-start = ((), (), s32[]{:S(2)}) async-start(), calls=%async_computation.19 | async-start | bytes 2359296 | tf_op jit(solution)/shard_map/all_gather | solution.py:194
  10.7 101.5 %all-gather.14.cloned.1.call-start = ((), (), s32[]{:S(2)}) async-start(), calls=%async_computation.12 | async-start | bytes 2359296 | tf_op jit(solution)/shard_map/all_gather | solution.py:194
  11.4 181.0 %reduce-scatter.17.cloned.1.call-start = ((), (), s32[]{:S(2)}) async-start(), calls=%async_computation.20 | async-start | bytes 4718592 | tf_op jit(solution)/shard_map/reduce_scatter | solution.py:203
  148.9 89.6 %reduce-scatter.13.cloned.1.call-start = ((), (), s32[]{:S(2)}) async-start(), calls=%async_computation.14 | async-start | bytes 4718592 | tf_op jit(solution)/shard_map/reduce_scatter | solution.py:203
  185.9 97.1 %all-gather.20.cloned.1.call-start = ((), (), s32[]{:S(2)}) async-start(), calls=%async_computation.16 | async-start | bytes 2506752 | tf_op jit(solution)/shard_map/all_gather | solution.py:188
  186.5 124.7 %all-gather.26.cloned.1.call-start = ((), (), s32[]{:S(2)}) async-start(), calls=%async_computation.21 | async-start | bytes 2359296 | tf_op jit(solution)/shard_map/all_gather | solution.py:217
  244.4 96.2 %all-gather.18.cloned.1.call-start = ((), (), s32[]{:S(2)}) async-start(), calls=%async_computation.15 | async-start | bytes 2359296 | tf_op jit(solution)/shard_map/all_gather | solution.py:217
  245.1 140.1 %all-gather.22.cloned.1.call-start = ((), (), s32[]{:S(2)}) async-start(), calls=%async_computation.17 | async-start | bytes 2506752 | tf_op jit(solution)/shard_map/all_gather | solution.py:189
  245.8 188.6 %reduce-scatter.15.cloned.1.call-start = ((), (), s32[]{:S(2)}) async-start(), calls=%async_computation.18 | async-start | bytes 4718592 | tf_op jit(solution)/shard_map/reduce_scatter | solution.py:221
  246.3 303.5 %copy-start.80 = (f32[1536]{0:T(1024)}, f32[1536]{0:T(1024)S(1)}, u32[]{:S(2)}) copy-start(f32[1536]{0:T(1024)S(1)} %add_divide_fusion) | copy-start | bytes 18436
  392.1 88.0 %reduce-scatter.19.cloned.1.call-start = ((), (), s32[]{:S(2)}) async-start(), calls=%async_computation.22 | async-start | bytes 4718592 | tf_op jit(solution)/shard_map/reduce_scatter | solution.py:221
  399.1 121.9 %all-gather.28.cloned.1.call-start = ((), (), s32[]{:S(2)}) async-start(), calls=%async_computation.23 | async-start | bytes 2359296 | tf_op jit(solution)/shard_map/all_gather | solution.py:239
  493.7 56.2 %all-gather.32.cloned.1.call-start = ((), (), s32[]{:S(2)}) async-start(), calls=%async_computation.27 | async-start | bytes 2359296 | tf_op jit(solution)/shard_map/all_gather | solution.py:239
  494.4 124.1 %reduce-scatter.25.cloned.1.call-start = ((), (), s32[]{:S(2)}) async-start(), calls=%async_computation.28 | async-start | bytes 4718592 | tf_op jit(solution)/shard_map/reduce_scatter | solution.py:247
  575.0 89.1 %reduce-scatter.21.cloned.1.call-start = ((), (), s32[]{:S(2)}) async-start(), calls=%async_computation.24 | async-start | bytes 4718592 | tf_op jit(solution)/shard_map/reduce_scatter | solution.py:247
  582.4 117.7 %all-gather.30.cloned.1.call-start = ((), (), s32[]{:S(2)}) async-start(), calls=%async_computation.25 | async-start | bytes 2359296 | tf_op jit(solution)/shard_map/all_gather | solution.py:253
  672.7 62.1 %all-gather.34.cloned.1.call-start = ((), (), s32[]{:S(2)}) async-start(), calls=%async_computation.29 | async-start | bytes 2359296 | tf_op jit(solution)/shard_map/all_gather | solution.py:253
  674.7 211.2 %reduce-scatter.23.cloned.1.call-start = ((), (), s32[]{:S(2)}) async-start(), calls=%async_computation.26 | async-start | bytes 2359296 | tf_op jit(solution)/shard_map/reduce_scatter | solution.py:268
  785.4 103.0 %reduce-scatter.27.cloned.1.call-start = ((), (), s32[]{:S(2)}) async-start(), calls=%async_computation.30 | async-start | bytes 2359296 | tf_op jit(solution)/shard_map/reduce_scatter | solution.py:268
  797.1 123.5 %reduce-scatter.35.cloned.1.call-start = ((), (), s32[]{:S(2)}) async-start(), calls=%async_computation.34 | async-start | bytes 5013504 | tf_op jit(solution)/shard_map/reduce_scatter | solution.py:290
  806.2 193.9 %reduce-scatter.33.cloned.1.call-start = ((), (), s32[]{:S(2)}) async-start(), calls=%async_computation.33 | async-start | bytes 5013504 | tf_op jit(solution)/shard_map/reduce_scatter | solution.py:289
  817.0 244.5 %reduce-scatter.31.cloned.1.call-start = ((), (), s32[]{:S(2)}) async-start(), calls=%async_computation.32 | async-start | bytes 1253376 | tf_op jit(solution)/shard_map/reduce_scatter | solution.py:288
  822.6 310.4 %reduce-scatter.29.cloned.1.call-start = ((), (), s32[]{:S(2)}) async-start(), calls=%async_computation.31 | async-start | bytes 3760128 | tf_op jit(solution)/shard_map/reduce_scatter | solution.py:287
  (151 other events, 1462.2 us)
Sparse Core Ops, SparseCore 0:
  10.3 44.1 all-gather.15
  56.6 26.1 all-gather.23
  84.9 27.2 all-gather.13
  149.0 43.3 reduce-scatter.16
  195.2 43.3 reduce-scatter.12
  240.7 42.3 all-gather.19
  285.1 25.9 all-gather.25
  313.3 27.2 all-gather.17
  342.8 42.3 all-gather.21
  392.2 42.1 reduce-scatter.14
  436.7 43.3 reduce-scatter.18
  493.8 27.1 all-gather.27
  522.6 27.2 all-gather.31
  575.1 43.3 reduce-scatter.24
  620.6 43.3 reduce-scatter.20
  672.8 27.2 all-gather.29
  701.5 27.2 all-gather.33
  785.5 26.0 reduce-scatter.22
  814.0 26.0 reduce-scatter.26
  844.4 76.1 reduce-scatter.34
  925.5 74.6 reduce-scatter.32
  1004.3 57.1 reduce-scatter.30
  1065.9 67.0 reduce-scatter.28
where the time goes:
time: 1150 us; the launch traced here: 1140 us
  waiting for transfers between devices  689 us (60%)
  matrix products  195 us (17%)
  local copies, waits for them, and re-layouts  96.9 us (8%)
  blocking collectives  75.9 us (7%)
  other arithmetic  60.8 us (5%)
  between operations  19.1 us (2%)
    reduce_scatter x2, waiting for transfers between devices, body(): lax.psum_scatter(matmul(g_pre_low, up_full, COLS_DIMS), 'tensor', scatter...  81.6 us
    reduce_scatter x2, waiting for transfers between devices, body(): lax.psum_scatter(matmul(activ_low, down_full, COLS_DIMS), 'tensor', scatt...  80.5 us
    reduce_scatter x1, waiting for transfers between devices, body(): lax.psum_scatter(big_sums[2], 'dp', scatter_dimension=0, tiled=True)  79.6 us
    reduce_scatter x1, waiting for transfers between devices, body(): lax.psum_scatter(big_sums[0], 'dp', scatter_dimension=0, tiled=True)  71.5 us
    dot_general x16, matrix products, matmul(): lax.dot_general(left, right, dims, preferred_element_type=jnp.float32)  68 us
    reduce_scatter x1, waiting for transfers between devices, body(): lax.psum_scatter(big_sums[1], 'dp', scatter_dimension=0, tiled=True)  61.3 us
    all_gather x2, waiting for transfers between devices, body(): spread = lax.all_gather(normed_low, 'tensor', axis=0, tiled=True)  50.1 us
    reduce_scatter x2, waiting for transfers between devices, body(): lax.psum_scatter(matmul(context, out_full, COLS_DIMS), 'tensor', scatter_...  50 us
  transfers between devices with their start and end apart: 23, of which 20 were waited for; matrix products, arithmetic and copies ran while one was open for 18% of the time, Pallas kernels for 0%

commit v1 on v0

v1 whole, which is shorter than its diff:
```python
import functools

import jax
import jax.numpy as jnp
from jax import lax
from jax.experimental import pallas as pl
from jax.experimental.pallas import tpu as pltpu
from jax.sharding import PartitionSpec as P

D = 768
HEADS = 12
HEAD_DIM = 64
FF = 3072
SEQ_LEN = 512
BETA = 2.0 / 3.0
EPS = 1e-12
NEG = -1e30
BF = jnp.bfloat16
F32 = jnp.float32
MESH = pl.DeviceIdType.MESH
VMEM_BYTES = 60 * 1024 * 1024
WIDTHS = (1152, 384, 1536, 1536)
ROW_BLOCK = 256
UNIT_BLOCK = 512
SMALL_ROWS = 24
NT = (((1,), (1,)), ((), ()))
TN = (((0,), (0,)), ((), ()))
NN = (((1,), (0,)), ((), ()))


def dot(left, right, dims=NN):
    return lax.dot_general(left, right, dims, preferred_element_type=F32)


def gate_values(noise, logit):
    return jax.nn.sigmoid((jnp.log(noise) - jnp.log1p(-noise) + logit) / BETA)


def vmem(n=1):
    return [pl.BlockSpec(memory_space=pltpu.VMEM)] * n


def hbm(n=1):
    return [pl.BlockSpec(memory_space=pl.ANY)] * n


def coords():
    dp = lax.axis_index("dp")
    return dp // 4, lax.rem(dp // 2, 2), lax.axis_index("tensor"), lax.rem(dp, 2)


def place(z, x, y, c):
    return ((z * 2 + x) * 2 + c, y)


def greet():
    z, x, y, c = coords()
    barrier = pltpu.get_barrier_semaphore()
    partners = [(lax.rem(z + k, 4), x, y, c) for k in (1, 2, 3)]
    partners += [(z, 1 - x, y, c), (z, x, 1 - y, c), (z, x, y, 1 - c)]
    for partner in partners:
        pl.semaphore_signal(barrier, inc=1, device_id=place(*partner), device_id_type=MESH)
    pl.semaphore_wait(barrier, len(partners))


class Gather:
    COPIES = 12
    PHASES = 5

    def __init__(self, chunks, ins, outs, local_sem, send_sem, recv_sem):
        self.chunks, self.ins, self.outs = chunks, ins, outs
        self.local_sem, self.send_sem, self.recv_sem = local_sem, send_sem, recv_sem
        self.kept = {}
        self.started = []
        self.locals = []
        self.step_at = 0

    def own(self):
        z, x, y, c = coords()
        for i, (src, dst) in enumerate(zip(self.ins, self.outs)):
            copy = pltpu.make_async_copy(src, dst.at[y, z, x, c], self.local_sem.at[i])
            copy.start()
            self.locals.append(copy)

    def send(self, chunk, slot, src, dst, target):
        copy = pltpu.make_async_remote_copy(
            src_ref=src,
            dst_ref=dst,
            send_sem=self.send_sem.at[chunk, slot],
            recv_sem=self.recv_sem.at[chunk, slot],
            device_id=place(*target),
            device_id_type=MESH,
        )
        copy.start()
        self.started.append(copy)
        self.kept[chunk, slot] = copy

    def arrived(self, chunk, *slots):
        for slot in slots:
            self.kept[chunk, slot].wait_recv()

    def phase(self, chunk, phase):
        z, x, y, c = coords()
        across, beside, core = (z, 1 - x, y, c), (z, x, 1 - y, c), (z, x, y, 1 - c)
        which, start, size = self.chunks[chunk]
        cols = pl.ds(start, size)
        out = self.outs[which]

        def pass_on(slot, view, target):
            self.send(chunk, slot, view, view, target)

        if phase == 0:
            for k in range(3):
                self.send(
                    chunk,
                    k,
                    self.ins[which].at[:, cols],
                    out.at[y, z, x, c, :, cols],
                    (lax.rem(z + k + 1, 4), x, y, c),
                )
        elif phase == 1:
            while self.locals:
                self.locals.pop().wait()
            self.arrived(chunk, 0, 1, 2)
            pass_on(3, out.at[y, 0:2, x, c, :, cols], across)
            pass_on(4, out.at[y, 2:4, x, c, :, cols], beside)
            pass_on(7, out.at[y, :, x, c, :, cols], core)
        elif phase == 2:
            self.arrived(chunk, 3)
            pass_on(5, out.at[y, 0:2, :, c, :, cols], beside)
            self.arrived(chunk, 4)
            pass_on(6, out.at[:, 2:4, x, c, :, cols], across)
            pass_on(8, out.at[y, 0:2, 1 - x, c, :, cols], core)
            pass_on(9, out.at[1 - y, 2:4, x, c, :, cols], core)
        elif phase == 3:
            self.arrived(chunk, 5)
            pass_on(10, out.at[1 - y, 0:2, :, c, :, cols], core)
            self.arrived(chunk, 6)
            pass_on(11, out.at[:, 2:4, 1 - x, c, :, cols], core)
        else:
            self.arrived(chunk, 7, 8, 9, 10, 11)

    def steps(self):
        return len(self.chunks) + self.PHASES - 1

    def step(self):
        if self.step_at < self.steps():
            for phase in range(self.PHASES):
                chunk = self.step_at - phase
                if 0 <= chunk < len(self.chunks):
                    self.phase(chunk, phase)
            self.step_at += 1

    def finish(self):
        while self.step_at < self.steps():
            self.step()
        for copy in self.started:
            copy.wait_send()


def gather_kernel(chunks, count, *refs):
    ins, outs = refs[:count], refs[count : 2 * count]
    gather = Gather(chunks, ins, outs, *refs[2 * count :])
    gather.own()
    greet()
    gather.finish()


def gather_call(chunks, shards):
    count, n = len(shards), len(chunks)
    outs = pl.pallas_call(
        functools.partial(gather_kernel, chunks, count),
        out_shape=[jax.ShapeDtypeStruct((2, 4, 2, 2, 48, s.shape[1]), BF) for s in shards],
        in_specs=hbm(count),
        out_specs=hbm(count),
        scratch_shapes=[
            pltpu.SemaphoreType.DMA((count,)),
            pltpu.SemaphoreType.DMA((n, Gather.COPIES)),
            pltpu.SemaphoreType.DMA((n, Gather.COPIES)),
        ],
        compiler_params=pltpu.CompilerParams(collective_id=1, has_side_effects=True),
        name="gather",
    )(*shards)
    return [o.reshape(2, D, o.shape[-1]) for o in outs]


class Scatter:
    COPIES = 8
    PHASES = 5

    def __init__(self, chunks, grads, outs, bufs, local_sem, send_sem, recv_sem):
        self.chunks, self.grads, self.outs, self.bufs = chunks, grads, outs, bufs
        self.local_sem, self.send_sem, self.recv_sem = local_sem, send_sem, recv_sem
        self.kept = {}
        self.started = []
        self.locals = {}
        self.step_at = 0

    def send(self, chunk, slot, src, dst, target):
        copy = pltpu.make_async_remote_copy(
            src_ref=src,
            dst_ref=dst,
            send_sem=self.send_sem.at[chunk, slot],
            recv_sem=self.recv_sem.at[chunk, slot],
            device_id=place(*target),
            device_id_type=MESH,
        )
        copy.start()
        self.started.append(copy)
        self.kept[chunk, slot] = copy

    def arrived(self, chunk, *slots):
        for slot in slots:
            self.kept[chunk, slot].wait_recv()

    def phase(self, chunk, phase):
        z, x, y, c = coords()
        across, beside, core = (z, 1 - x, y, c), (z, x, 1 - y, c), (z, x, y, 1 - c)
        which, start, size = self.chunks[chunk]
        cols = pl.ds(start, size)
        grad = self.grads[which]
        sums, first, low_a, low_b, next_a, next_b, last_a, last_b, mine, last = self.bufs[chunk]

        def add(dst, left, right):
            dst[...] = (left[...].astype(F32) + right[...].astype(F32)).astype(BF)

        if phase == 0:
            self.send(chunk, 0, grad.at[:, :, :, 1 - c, :, cols], first, core)
            copy = pltpu.make_async_copy(
                grad.at[:, :, :, c, :, cols], sums, self.local_sem.at[chunk]
            )
            copy.start()
            self.locals[chunk] = copy
        elif phase == 1:
            self.locals[chunk].wait()
            self.arrived(chunk, 0)

            @pl.loop(0, 16)
            def _(i):
                at = (i // 8, lax.rem(i // 2, 4), lax.rem(i, 2))
                add(sums.at[at], sums.at[at], first.at[at])

            self.send(chunk, 1, sums.at[1 - y, 0:2], low_a, beside)
            self.send(chunk, 2, sums.at[:, 2:4, 1 - x], low_b, across)
        elif phase == 2:
            self.arrived(chunk, 1)

            @pl.loop(0, 4)
            def _(i):
                at = (i // 2, lax.rem(i, 2))
                add(next_a.at[at], sums.at[(y,) + at], low_a.at[at])

            self.send(chunk, 3, next_a.at[:, 1 - x], last_a, across)
            self.arrived(chunk, 2)

            @pl.loop(0, 4)
            def _(i):
                t, k = i // 2, lax.rem(i, 2)
                add(next_b.at[t, k], sums.at[t, k + 2, x], low_b.at[t, k])

            self.send(chunk, 4, next_b.at[1 - y], last_b, beside)
        elif phase == 3:
            self.arrived(chunk, 3, 4)

            @pl.loop(0, 2)
            def _(k):
                add(mine.at[k], next_a.at[k, x], last_a.at[k])
                add(mine.at[k + 2], next_b.at[y, k], last_b.at[k])

            for k in range(3):
                to = lax.rem(z + k + 1, 4)
                self.send(chunk, 5 + k, mine.at[to], last.at[k], (to, x, y, c))
        else:
            self.arrived(chunk, 5, 6, 7)
            total = mine[z].astype(F32)
            for k in range(3):
                total = total + last[k].astype(F32)
            self.outs[which][:, cols] = total

    def steps(self):
        return len(self.chunks) + self.PHASES - 1

    def step(self):
        if self.step_at < self.steps():
            for phase in range(self.PHASES):
                chunk = self.step_at - phase
                if 0 <= chunk < len(self.chunks):
                    self.phase(chunk, phase)
            self.step_at += 1

    def finish(self):
        while self.step_at < self.steps():
            self.step()
        for copy in self.started:
            copy.wait_send()

    @staticmethod
    def scratch(chunks):
        shapes = []
        for _, _, n in chunks:
            shapes += [
                pltpu.VMEM((2, 4, 2, 48, n), BF),
                pltpu.VMEM((2, 4, 2, 48, n), BF),
                pltpu.VMEM((2, 2, 48, n), BF),
                pltpu.VMEM((2, 2, 48, n), BF),
                pltpu.VMEM((2, 2, 48, n), BF),
                pltpu.VMEM((2, 2, 48, n), BF),
                pltpu.VMEM((2, 48, n), BF),
                pltpu.VMEM((2, 48, n), BF),
                pltpu.VMEM((4, 48, n), BF),
                pltpu.VMEM((3, 48, n), BF),
            ]
        return shapes

    @staticmethod
    def semaphores(chunks):
        n = len(chunks)
        return [
            pltpu.SemaphoreType.DMA((n,)),
            pltpu.SemaphoreType.DMA((n, Scatter.COPIES)),
            pltpu.SemaphoreType.DMA((n, Scatter.COPIES)),
        ]


class Small:
    def __init__(self, out, own, got, lines, send_sem, recv_sem):
        self.out, self.own, self.got, self.lines = out, own, got, lines
        self.send_sem, self.recv_sem = send_sem, recv_sem
        self.pending = []
        self.step_at = 0

    def send(self, slot, src, dst, target):
        copy = pltpu.make_async_remote_copy(
            src_ref=src,
            dst_ref=dst,
            send_sem=self.send_sem.at[slot],
            recv_sem=self.recv_sem.at[slot],
            device_id=place(*target),
            device_id_type=MESH,
        )
        copy.start()
        self.pending.append(copy)

    def step(self):
        z, x, y, c = coords()
        nearby = ((z, x, y, 1 - c), (z, 1 - x, y, c), (z, x, 1 - y, c))
        at = self.step_at
        if at > 4:
            return
        self.step_at += 1
        for copy in self.pending:
            copy.wait()
        self.pending = []
        if 1 <= at <= 3:
            self.own[at] = self.own[at - 1] + self.got[at - 1]
        if at < 3:
            self.send(at, self.own.at[at], self.got.at[at], nearby[at])
        elif at == 3:
            self.lines[z] = self.own[3]
            for k in range(3):
                to = (lax.rem(z + k + 1, 4), x, y, c)
                self.send(3 + k, self.own.at[3], self.lines.at[z], to)
        else:
            self.out[...] = (self.lines[0] + self.lines[1]) + (self.lines[2] + self.lines[3])

    def finish(self):
        while self.step_at <= 4:
            self.step()

    @staticmethod
    def scratch():
        return [
            pltpu.VMEM((4, SMALL_ROWS, D), F32),
            pltpu.VMEM((3, SMALL_ROWS, D), F32),
            pltpu.VMEM((4, SMALL_ROWS, D), F32),
            pltpu.SemaphoreType.DMA((6,)),
            pltpu.SemaphoreType.DMA((6,)),
        ]


def scatter_kernel(chunks, count, *refs):
    grads, small_a, small_b = refs[:count], refs[count], refs[count + 1]
    refs = refs[count + 2 :]
    outs, small_out = refs[:count], refs[count]
    refs = refs[count + 1 :]
    bufs = [refs[10 * i : 10 * i + 10] for i in range(len(chunks))]
    refs = refs[10 * len(chunks) :]
    scatter = Scatter(chunks, grads, outs, bufs, *refs[:3])
    small = Small(small_out, *refs[3:])
    small.own[0] = small_a[...] + small_b[...]
    greet()
    while scatter.step_at < scatter.steps():
        scatter.step()
        small.step()
    small.finish()
    scatter.finish()


def scatter_call(chunks, grads, small_a, small_b):
    count = len(grads)
    grads = [g.reshape(2, 4, 2, 2, 48, g.shape[-1]) for g in grads]
    return pl.pallas_call(
        functools.partial(scatter_kernel, chunks, count),
        out_shape=[jax.ShapeDtypeStruct((48, g.shape[-1]), F32) for g in grads]
        + [jax.ShapeDtypeStruct((SMALL_ROWS, D), F32)],
        in_specs=hbm(count) + vmem(2),
        out_specs=vmem(count + 1),
        scratch_shapes=Scatter.scratch(chunks) + Scatter.semaphores(chunks) + Small.scratch(),
        compiler_params=pltpu.CompilerParams(
            collective_id=2, has_side_effects=True, vmem_limit_bytes=VMEM_BYTES
        ),
        name="scatter",
    )(*grads, small_a, small_b)


def head_masks():
    lane = lax.broadcasted_iota(jnp.int32, (SEQ_LEN, 128), 1)
    return lane < HEAD_DIM


def pair_at(i):
    seq, pair = i // 6, lax.rem(i, 6)
    half, col = pair // 3, lax.rem(pair, 3)
    return seq, half, col, pl.ds(pl.multiple_of(seq * SEQ_LEN, SEQ_LEN), SEQ_LEN)


def lanes(col, base):
    return pl.ds(pl.multiple_of(base + col * 128, 128), 128)


def mask_into(bias, marks_ref, marks_col_ref):
    for s in range(bias.shape[0]):
        same = marks_col_ref[s] == marks_ref[s : s + 1, :]
        bias[s] = jnp.where(same, 0.0, NEG)


def forward_kernel(
    tokens, qkv, out_w, affine, marks, marks_col, mix, context, lse, attn, bias
):
    mask_into(bias, marks, marks_col)
    rows_all = tokens.shape[0]

    @pl.loop(0, rows_all // ROW_BLOCK)
    def _(i):
        rows = pl.ds(pl.multiple_of(i * ROW_BLOCK, ROW_BLOCK), ROW_BLOCK)
        for t in range(2):
            mixed = dot(tokens[rows, :], qkv[t])
            mix[t, rows, :] = ((mixed + affine[t, 0:1, :]) * affine[t, 1:2, :]).astype(BF)

    left = head_masks()

    @pl.loop(0, 12)
    def _(i):
        seq, t, col, rows = pair_at(i)
        query = mix[t, rows, lanes(col, 0)]
        keys = mix[t, rows, lanes(col, 384)]
        values = mix[t, rows, lanes(col, 768)]
        parts = []
        for h in range(2):
            mine = jnp.where(left if h == 0 else ~left, query, 0)
            scores = dot(mine, keys, NT) + bias[seq]
            top = jnp.max(scores, axis=1, keepdims=True)
            expo = jnp.exp(scores - top)
            total = jnp.sum(expo, axis=1, keepdims=True)
            probs = (expo * (1.0 / total)).astype(BF)
            parts.append(dot(probs, values))
            logsum = jnp.broadcast_to(top + jnp.log(total), (SEQ_LEN, 128))
            lse[i, h : h + 1, :] = jnp.transpose(logsum)[0:1, :]
        context[t, rows, lanes(col, 0)] = jnp.where(left, parts[0], parts[1]).astype(BF)

    @pl.loop(0, rows_all // ROW_BLOCK)
    def _(i):
        rows = pl.ds(pl.multiple_of(i * ROW_BLOCK, ROW_BLOCK), ROW_BLOCK)
        attn[rows, :] = dot(context[0, rows, :], out_w[0], NT) + dot(
            context[1, rows, :], out_w[1], NT
        )


def forward_call(tokens, qkv, out_w, affine, marks, marks_col):
    rows = tokens.shape[0]
    seqs = rows // SEQ_LEN
    return pl.pallas_call(
        forward_kernel,
        out_shape=[
            jax.ShapeDtypeStruct((2, rows, 1152), BF),
            jax.ShapeDtypeStruct((2, rows, 384), BF),
            jax.ShapeDtypeStruct((6 * seqs, 8, SEQ_LEN), F32),
            jax.ShapeDtypeStruct((rows, D), F32),
        ],
        in_specs=vmem(6),
        out_specs=vmem(4),
        scratch_shapes=[pltpu.VMEM((seqs, SEQ_LEN, SEQ_LEN), F32)],
        compiler_params=pltpu.CompilerParams(vmem_limit_bytes=VMEM_BYTES),
        name="attention_forward",
    )(tokens, qkv, out_w, affine, marks, marks_col)


def backward_kernel(
    tokens,
    qkv,
    out_w,
    affine,
    marks,
    marks_col,
    mix,
    context,
    lse,
    g_attn,
    g_resid,
    tokens_grad,
    qkv_grad,
    out_grad,
    small,
    bias,
    g_context,
    g_mix,
    tokens_t,
    g_attn_t,
    head_sum,
):
    mask_into(bias, marks, marks_col)
    rows_all = tokens.shape[0]
    head_sum[...] = jnp.zeros_like(head_sum)

    @pl.loop(0, rows_all // ROW_BLOCK)
    def _(i):
        rows = pl.ds(pl.multiple_of(i * ROW_BLOCK, ROW_BLOCK), ROW_BLOCK)
        for t in range(2):
            g_context[t, rows, :] = dot(g_attn[rows, :], out_w[t]).astype(BF)

    for i in range(rows_all // ROW_BLOCK):
        rows = slice(i * ROW_BLOCK, (i + 1) * ROW_BLOCK)
        tokens_t[:, rows] = jnp.transpose(tokens[rows, :])
        g_attn_t[:, rows] = jnp.transpose(g_attn[rows, :])
    for t in range(2):
        out_grad[t] = dot(g_attn_t[...], context[t]).astype(BF)

    left = head_masks()

    @pl.loop(0, 12)
    def _(i):
        seq, t, col, rows = pair_at(i)
        query = mix[t, rows, lanes(col, 0)]
        keys = mix[t, rows, lanes(col, 384)]
        values = mix[t, rows, lanes(col, 768)]
        grad = g_context[t, rows, lanes(col, 0)]
        parts = []
        for h in range(2):
            side = left if h == 0 else ~left
            scores = dot(jnp.where(side, keys, 0), query, NT) + bias[seq]
            probs = jnp.exp(scores - lse[i, h : h + 1, :])
            g_probs = dot(jnp.where(side, values, 0), grad, NT)
            delta = jnp.sum(g_probs * probs, axis=0, keepdims=True)
            g_scores = (probs * (g_probs - delta)).astype(BF)
            parts.append(
                (
                    dot(g_scores, keys, TN),
                    dot(g_scores, query),
                    dot(probs.astype(BF), grad),
                )
            )
        g_query, g_keys, g_values = (jnp.where(left, a, b) for a, b in zip(*parts))
        g_mix[t, rows, lanes(col, 0)] = (g_query * HEAD_DIM**-0.5).astype(BF)
        g_mix[t, rows, lanes(col, 384)] = g_keys.astype(BF)
        v_lanes = lanes(col, 768)
        g_mix[t, rows, v_lanes] = (g_values * affine[t, 1:2, v_lanes]).astype(BF)
        used = jnp.sum(g_values * values.astype(F32), axis=0, keepdims=True)
        head_sum[t, 0:1, lanes(col, 0)] += used

    small[...] = jnp.zeros_like(small)
    ones = jnp.ones((8, rows_all), BF)
    for t in range(2):
        at = slice(384 * t, 384 * (t + 1))
        sums = dot(ones, g_mix[t])
        small[17:18, at] = sums[0:1, 0:384]
        small[18:19, at] = sums[0:1, 768:1152]
        small[19:20, at] = head_sum[t, 0:1, :] / affine[t, 1:2, 768:1152]
        for k in range(3):
            cols = slice(384 * k, 384 * (k + 1))
            qkv_grad[t, :, cols] = dot(tokens_t[...], g_mix[t, :, cols]).astype(BF)

    @pl.loop(0, rows_all // ROW_BLOCK)
    def _(i):
        rows = pl.ds(pl.multiple_of(i * ROW_BLOCK, ROW_BLOCK), ROW_BLOCK)
        tokens_grad[rows, :] = g_resid[rows, :] + (
            dot(g_mix[0, rows, :], qkv[0], NT) + dot(g_mix[1, rows, :], qkv[1], NT)
        )


def backward_call(tokens, qkv, out_w, affine, marks, marks_col, mix, context, lse, g_attn, g_resid):
    rows = tokens.shape[0]
    seqs = rows // SEQ_LEN
    return pl.pallas_call(
        backward_kernel,
        out_shape=[
            jax.ShapeDtypeStruct((rows, D), F32),
            jax.ShapeDtypeStruct((2, D, 1152), BF),
            jax.ShapeDtypeStruct((2, D, 384), BF),
            jax.ShapeDtypeStruct((SMALL_ROWS, D), F32),
        ],
        in_specs=vmem(11),
        out_specs=vmem(4),
        scratch_shapes=[
            pltpu.VMEM((seqs, SEQ_LEN, SEQ_LEN), F32),
            pltpu.VMEM((2, rows, 384), BF),
            pltpu.VMEM((2, rows, 1152), BF),
            pltpu.VMEM((D, rows), BF),
            pltpu.VMEM((D, rows), BF),
            pltpu.VMEM((2, 8, 384), F32),
        ],
        compiler_params=pltpu.CompilerParams(vmem_limit_bytes=VMEM_BYTES),
        name="attention_backward",
    )(tokens, qkv, out_w, affine, marks, marks_col, mix, context, lse, g_attn, g_resid)


def normalise(value):
    mean = jnp.mean(value, axis=1, keepdims=True)
    centred = value - mean
    var = jnp.mean(centred * centred, axis=1, keepdims=True)
    rstd = lax.rsqrt(var + EPS)
    return centred * rstd, rstd


def norm_back(grad, unit, rstd):
    mean = jnp.mean(grad, axis=1, keepdims=True)
    along = jnp.mean(grad * unit, axis=1, keepdims=True)
    return rstd * (grad - mean - unit * along)


def fold(value):
    return jnp.sum(value.reshape(value.shape[0] // 8, 8, value.shape[1]), axis=0)


def feed_kernel(
    tokens,
    teacher,
    attn,
    up_w,
    down_w,
    vec,
    uvec,
    activations,
    g_attn,
    g_resid,
    up_grad,
    down_grad,
    small,
    pre_deriv,
    activ,
    g_pre,
    normed_t,
    g_ffn_t,
    sums,
    unit_sums,
):
    rows_all = tokens.shape[0]
    sums[...] = jnp.zeros_like(sums)
    unit_sums[...] = jnp.zeros_like(unit_sums)
    out_bias, scale1, gain1, shift1 = (vec[i : i + 1, :] for i in range(4))
    down_bias, scale2, gain2, shift2 = (vec[i : i + 1, :] for i in range(4, 8))
    per = 1536 // UNIT_BLOCK

    @pl.loop(0, rows_all // ROW_BLOCK)
    def _(i):
        rows = pl.ds(pl.multiple_of(i * ROW_BLOCK, ROW_BLOCK), ROW_BLOCK)
        attn_b = attn[rows, :] + out_bias
        unit1, rstd1 = normalise(tokens[rows, :].astype(F32) + attn_b * scale1)
        normed = unit1 * gain1 + shift1
        normed_low = normed.astype(BF)
        normed_t[:, rows] = jnp.transpose(normed_low)
        ffn = jnp.zeros((ROW_BLOCK, D), F32)
        for j in range(2 * per):
            t, cols = j // per, slice((j % per) * UNIT_BLOCK, (j % per + 1) * UNIT_BLOCK)
            flat = slice(j * UNIT_BLOCK, (j + 1) * UNIT_BLOCK)
            pre = dot(normed_low, up_w[t, :, cols]) + uvec[0:1, flat]
            gate = uvec[1:2, flat]
            phi = 0.5 + 0.5 * lax.erf(pre * (0.5**0.5))
            pdf = jnp.exp(pre * pre * -0.5) * ((2.0 * jnp.pi) ** -0.5)
            act = (pre * phi * gate).astype(BF)
            pre_deriv[:, flat] = (phi + pre * pdf) * gate
            activ[rows, flat] = act
            ffn = ffn + dot(act, down_w[t, :, cols], NT)
        ffn_b = ffn + down_bias
        unit2, rstd2 = normalise(normed + ffn_b * scale2)
        result = unit2 * gain2 + shift2
        activations[rows, :] = result.astype(BF)
        diff = result - teacher[rows, :].astype(F32)
        g_value2 = norm_back(diff * gain2, unit2, rstd2)
        g_ffn_low = (g_value2 * scale2).astype(BF)
        g_ffn_t[:, rows] = jnp.transpose(g_ffn_low)
        sums[2] += fold(g_value2)
        sums[3] += fold(g_value2 * ffn_b)
        sums[6] += fold(diff * unit2)
        sums[7] += fold(diff)
        sums[8] += fold(diff * diff)
        g_normed = g_value2
        for j in range(2 * per):
            t, cols = j // per, slice((j % per) * UNIT_BLOCK, (j % per + 1) * UNIT_BLOCK)
            flat = slice(j * UNIT_BLOCK, (j + 1) * UNIT_BLOCK)
            g_activ = dot(g_ffn_low, down_w[t, :, cols])
            unit_sums[:, flat] += fold(g_activ * activ[rows, flat].astype(F32))
            grad = (g_activ * pre_deriv[:, flat]).astype(BF)
            g_pre[rows, flat] = grad
            g_normed = g_normed + dot(grad, up_w[t, :, cols], NT)
        g_value1 = norm_back(g_normed * gain1, unit1, rstd1)
        g_resid[rows, :] = g_value1
        g_attn[rows, :] = (g_value1 * scale1).astype(BF)
        sums[0] += fold(g_value1)
        sums[1] += fold(g_value1 * attn_b)
        sums[4] += fold(g_normed * unit1)
        sums[5] += fold(g_normed)

    small[...] = jnp.zeros_like(small)
    for k in range(9):
        small[k : k + 1, :] = jnp.sum(sums[k], axis=0, keepdims=True)
    ones = jnp.ones((8, rows_all), BF)
    for j in range(4):
        cols = slice(768 * j, 768 * (j + 1))
        small[9 + j : 10 + j, :] = dot(ones, g_pre[:, cols])[0:1, :]
        total = jnp.sum(unit_sums[:, cols], axis=0, keepdims=True)
        small[13 + j : 14 + j, :] = total / uvec[1:2, cols]

    @pl.loop(0, FF // UNIT_BLOCK)
    def _(j):
        t = j // per
        flat = pl.ds(pl.multiple_of(j * UNIT_BLOCK, UNIT_BLOCK), UNIT_BLOCK)
        cols = pl.ds(pl.multiple_of(lax.rem(j, per) * UNIT_BLOCK, UNIT_BLOCK), UNIT_BLOCK)
        down_grad[t, :, cols] = dot(g_ffn_t[...], activ[:, flat]).astype(BF)
        up_grad[t, :, cols] = dot(normed_t[...], g_pre[:, flat]).astype(BF)


def feed_call(tokens, teacher, attn, up_w, down_w, vec, uvec):
    rows = tokens.shape[0]
    return pl.pallas_call(
        feed_kernel,
        out_shape=[
            jax.ShapeDtypeStruct((rows, D), BF),
            jax.ShapeDtypeStruct((rows, D), BF),
            jax.ShapeDtypeStruct((rows, D), F32),
            jax.ShapeDtypeStruct((2, D, 1536), BF),
            jax.ShapeDtypeStruct((2, D, 1536), BF),
            jax.ShapeDtypeStruct((SMALL_ROWS, D), F32),
        ],
        in_specs=vmem(7),
        out_specs=vmem(6),
        scratch_shapes=[
            pltpu.VMEM((ROW_BLOCK, FF), F32),
            pltpu.VMEM((rows, FF), BF),
            pltpu.VMEM((rows, FF), BF),
            pltpu.VMEM((D, rows), BF),
            pltpu.VMEM((D, rows), BF),
            pltpu.VMEM((9, 8, D), F32),
            pltpu.VMEM((8, FF), F32),
        ],
        compiler_params=pltpu.CompilerParams(vmem_limit_bytes=VMEM_BYTES),
        name="feed_forward",
    )(tokens, teacher, attn, up_w, down_w, vec, uvec)


GATHER_CHUNKS = (
    (0, 0, 1152),
    (1, 0, 384),
    (2, 0, 768),
    (2, 768, 768),
    (3, 0, 768),
    (3, 768, 768),
)
SCATTER_CHUNKS = (
    (3, 0, 768),
    (3, 768, 768),
    (2, 0, 768),
    (2, 768, 768),
    (1, 0, 384),
    (0, 0, 1152),
)


def body(
    direct,
    tokens,
    teacher,
    segments,
    qkv_weight,
    qkv_bias,
    out_weight,
    out_bias,
    up_weight,
    up_bias,
    down_weight,
    down_bias,
    first_gain,
    first_shift,
    second_gain,
    second_shift,
    head_logit,
    unit_logit,
    width_logit,
    layer_logit,
    head_noise,
    unit_noise,
    width_noise,
    layer_noise,
):
    z_head = gate_values(head_noise, head_logit)
    z_unit = gate_values(unit_noise, unit_logit)
    z_width = gate_values(width_noise, width_logit)
    z_layer = gate_values(layer_noise, layer_logit)
    shards = (qkv_weight.reshape(-1, 1152), out_weight, up_weight, down_weight)
    if direct:
        full = gather_call(GATHER_CHUNKS, shards)
    else:
        full = [
            lax.all_gather(lax.all_gather(s, "dp", axis=0, tiled=True), "tensor", axis=0)
            for s in shards
        ]
    qkv_full, out_full, up_full, down_full = full
    by_half = lambda v: v.reshape(2, 384)
    zh = by_half(jnp.repeat(z_head, HEAD_DIM))
    zeros, ones = jnp.zeros((2, 384), F32), jnp.ones((2, 384), F32)
    affine = jnp.stack(
        [
            jnp.concatenate([by_half(qkv_bias[0]), zeros, by_half(qkv_bias[1])], axis=1),
            jnp.concatenate([ones * HEAD_DIM**-0.5, ones, zh], axis=1),
        ],
        axis=1,
    )
    scale1, scale2 = z_layer[0] * z_width, z_layer[1] * z_width
    vec = jnp.stack(
        [
            out_bias,
            scale1,
            first_gain,
            first_shift,
            down_bias,
            scale2,
            second_gain,
            second_shift,
        ]
    )
    uvec = jnp.stack([up_bias, z_unit])
    marks, marks_col = segments, segments[:, :, None]
    mix, context, lse, attn = forward_call(tokens, qkv_full, out_full, affine, marks, marks_col)
    activations, g_attn, g_resid, up_grad, down_grad, small_a = feed_call(
        tokens, teacher, attn, up_full, down_full, vec, uvec
    )
    tokens_grad, qkv_grad, out_grad, small_b = backward_call(
        tokens, qkv_full, out_full, affine, marks, marks_col, mix, context, lse, g_attn, g_resid
    )
    grads = (qkv_grad, out_grad, up_grad, down_grad)
    if direct:
        *grads, small = scatter_call(SCATTER_CHUNKS, grads, small_a, small_b)
    else:
        grads = [
            lax.psum_scatter(
                lax.psum_scatter(g, "tensor", scatter_dimension=0),
                "dp",
                scatter_dimension=0,
                tiled=True,
            ).astype(F32)
            for g in grads
        ]
        small = lax.psum(small_a + small_b, ("dp", "tensor"))
    qkv_grad, out_grad, up_grad, down_grad = grads
    slope = lambda gate: gate * (1.0 - gate) * 1.5
    all_tokens = tokens.shape[0] * lax.axis_size("dp") * lax.axis_size("tensor")
    width_grad = (small[1] * z_layer[0] + small[3] * z_layer[1]) * slope(z_width)
    layer_grad = jnp.stack([jnp.sum(small[1] * z_width), jnp.sum(small[3] * z_width)])
    return (
        activations,
        0.5 * jnp.sum(small[8]) / all_tokens,
        tokens_grad,
        qkv_grad.reshape(-1, 3, 384),
        small[17:19],
        out_grad,
        small[0] * scale1,
        up_grad,
        small[9:13].reshape(FF),
        down_grad,
        small[2] * scale2,
        small[4],
        small[5],
        small[6],
        small[7],
        jnp.sum(small[19].reshape(HEADS, HEAD_DIM), axis=1) * slope(z_head),
        small[13:17].reshape(FF) * slope(z_unit),
        width_grad,
        layer_grad * slope(z_layer),
    )


def solution(mesh):
    rows, split, whole = P(("dp", "tensor"), None), P("dp", "tensor"), P()
    cube = P("dp", None, "tensor")
    in_specs = (rows, rows, rows, cube, whole, split, whole, split, whole, split) + (whole,) * 13
    out_specs = (
        rows,
        whole,
        rows,
        cube,
        whole,
        split,
        whole,
        split,
        whole,
        split,
    ) + (whole,) * 9
    direct = mesh.shape["dp"] == 16 and mesh.shape["tensor"] == 2
    return jax.shard_map(
        functools.partial(body, direct),
        mesh=mesh,
        in_specs=in_specs,
        out_specs=out_specs,
        check_vma=False,
    )
```

time: 1150 us -> 328 us (0.29)
  waiting for transfers between devices: 689 us -> 0 us
  Pallas kernels: 0 us -> 290 us
  matrix products: 195 us -> 0 us
  local copies, waits for them, and re-layouts: 96.9 us -> 19.1 us
  blocking collectives: 75.9 us -> 0 us
  other arithmetic: 60.8 us -> 15.5 us
  between operations: 19.1 us -> 2.55 us
    reduce_scatter x12 -> x0, waiting for transfers between devices: 453 us -> none  [the longest x2 81.6 us: body(): lax.psum_scatter(matmul(g_pre_low, up_full, COLS_DIMS), 'tensor', scatter...]
    pallas_call x0 -> x5, Pallas kernels: none -> 290 us  [the longest x1 79.4 us: scatter_call(): pl.pallas_call(functools.partial(scatter_kernel, chunks, count), out_shap...]
    all_gather x11 -> x0, waiting for transfers between devices: 232 us -> none  [the longest x2 50.1 us: body(): spread = lax.all_gather(normed_low, 'tensor', axis=0, tiled=True)]
    dot_general x52 -> x0, matrix products: 195 us -> none  [the longest x16 68 us: matmul(): lax.dot_general(left, right, dims, preferred_element_type=jnp.float32)]
    psum x1 -> x0, blocking collectives: 41.5 us -> none  [body(): lax.psum((qkv_bias_place, up_bias_place, head_place, unit_place, sum_out_...]
    all_gather x3 -> x0, blocking collectives: 34.4 us -> none  [the longest x1 24.6 us: body(): lax.all_gather(shards[1], 'dp', axis=0, tiled=True)]
    reduce_sum x22 -> x2, other arithmetic: 35.7 us -> 2.61 us  [the longest x1 2.49 us: body(): jnp.sum(small[1] * z_width)]
    while x52 -> x0, local copies, waits for them, and re-layouts: 21.3 us -> none  [the longest x8 10.1 us: forward_attention(): lax.map(forward_single, (head_shape(query, marks), head_shape(keys, marks...]
  transfers between devices with their start and end apart: 23 -> 0, of which waited for: 20 -> 0; matrix products, arithmetic and copies ran while one was open for 18% -> 0% of each run, Pallas kernels for 0% -> 0%
where the time goes in v1:
time: 328 us; the launch traced here: 327 us
  Pallas kernels  290 us (88%)
  local copies, waits for them, and re-layouts  19.1 us (6%)
  other arithmetic  15.5 us (5%)
    pallas_call x1, Pallas kernels, scatter_call(): pl.pallas_call(functools.partial(scatter_kernel, chunks, count), out_shap...  79.4 us
    pallas_call x1, Pallas kernels, gather_call(): pl.pallas_call(functools.partial(gather_kernel, chunks, count), out_shape...  79 us
    pallas_call x1, Pallas kernels, feed_call(): pl.pallas_call(feed_kernel, out_shape=[jax.ShapeDtypeStruct((rows, D), BF...  52.7 us
    pallas_call x1, Pallas kernels, backward_call(): pl.pallas_call(backward_kernel, out_shape=[jax.ShapeDtypeStruct((rows, D)...  49.6 us
    pallas_call x1, Pallas kernels, forward_call(): pl.pallas_call(forward_kernel, out_shape=[jax.ShapeDtypeStruct((2, rows,...  29.6 us

profile of v1, /device:TPU:0, one launch (start us, length us, event | category | flops | bytes accessed | tf_op | source)
XLA Modules:
  0.0 327.4 jit_solution(12255574728994715130)
XLA Ops:
  1.3 0.7 add_divide_fusion.2
  3.4 0.7 stack.61
  5.5 0.7 stack.63
  7.1 1.4 broadcast_multiply_fusion
  9.8 0.8 slice_reduce_fusion.11
  11.2 0.7 add_divide_fusion
  12.0 1.3 pad_maximum_fusion.uvec
  13.3 1.6 copy.49
  14.9 1.7 copy.45.marks_col
  16.6 79.0 %gather.1 = (bf16[2,4,2,2,48,1152]{5,4,3,2,1,0:T(8,128)(2,1)}, bf16[2,4,2,2,48,384]{5,4,3,2,1,0:T(8,128)(2,1)}, bf16[2,4,2,2,48,1536]{5,4,3,2,1,0:T(8,128)(2,1)}, bf16[2,4,2,2,48,1536]{5,4,3,2,1,0:T(8,128)(2,1)}) custom-call(bf16[48,1152]{1,0:T(8,128)(2,1)} %bitcast.31, bf16[48,384]{1,0:T(8,128)(2,1)} %refs_1_.1, bf16[48,1536]{1,0:T(8,128)(2,1)} %refs_2_.1, ...), custom_call_target="tpu_custom_call" | custom-call | tf_op jit(solution)/shard_map/gather/pallas_call | solution.py:171
  95.6 29.6 %attention_forward.1 = (bf16[2,1024,1152]{2,1,0:T(8,128)(2,1)}, bf16[2,1024,384]{2,1,0:T(8,128)(2,1)}, f32[12,8,512]{2,1,0:T(8,128)}, f32[1024,768]{1,0:T(8,128)}) custom-call(bf16[1024,768]{1,0:T(8,128)(2,1)} %tokens.5, bf16[2,768,1152]{2,1,0:T(8,128)(2,1)} %bitcast.21, bf16[2,768,384]{2,1,0:T(8,128)(2,1)} %bitcast.25, ...), custom_call_target="tpu_custom_call" | custom-call | tf_op jit(solution)/shard_map/attention_forward/pallas_call | solution.py:482
  125.3 52.7 %feed_forward.1 = (bf16[1024,768]{1,0:T(8,128)(2,1)}, bf16[1024,768]{1,0:T(8,128)(2,1)}, f32[1024,768]{1,0:T(8,128)}, bf16[2,768,1536]{2,1,0:T(8,128)(2,1)}, bf1...) custom-call(bf16[1024,768]{1,0:T(8,128)(2,1)} %tokens.5, bf16[1024,768]{1,0:T(8,128)(2,1)} %teacher.1, ...), custom_call_target="tpu_custom_call" | custom-call | tf_op jit(solution)/shard_map/feed_forward/pallas_call | solution.py:734
  178.0 49.6 %attention_backward.1 = (f32[1024,768]{1,0:T(8,128)}, bf16[2,768,1152]{2,1,0:T(8,128)(2,1)}, bf16[2,768,384]{2,1,0:T(8,128)(2,1)}, f32[24,768]{1,0:T(8,128)}) custom-call(bf16[1024,768]{1,0:T(8,128)(2,1)} %tokens.5, bf16[2,768,1152]{2,1,0:T(8,128)(2,1)} %bitcast.22, bf16[2,768,384]{2,1,0:T(8,128)(2,1)} %bitcast.26, f32[2,2,1152]{2,1,0:T(2,128)} %pad_maximum_fusion.1.affine, ...), custom_call_target="tpu_custom_call" | custom-call | tf_op jit(solution)/shard_map/attention_backward/pallas_call | solution.py:593
  227.5 79.4 %scatter.1 = (f32[48,1152]{1,0:T(8,128)}, f32[48,384]{1,0:T(8,128)}, f32[48,1536]{1,0:T(8,128)}, f32[48,1536]{1,0:T(8,128)}, f32[24,768]{1,0:T(8,128)}) custom-call(bf16[2,4,2,2,48,1152]{5,4,3,2,1,0:T(8,128)(2,1)} %bitcast.29, bf16[2,4,2,2,48,384]{5,4,3,2,1,0:T(8,128)(2,1)} %bitcast.30, bf16[2,4,2,2,48,1536]{5,4,3,2,1,0:T(8,128)(2,1)} %bitcast.27, ...), custom_call_target="tpu_custom_call" | custom-call | tf_op jit(solution)/shard_map/scatter/pallas_call | solution.py:402
  306.9 1.6 copy.51
  308.5 1.3 slice.60
  309.9 0.8 fusion.8
  310.7 1.9 slice_reduce_fusion.1
  313.8 2.5 multiply_reduce_fusion.1
  316.3 1.2 fusion.10
  317.6 1.9 fusion.7
  321.4 1.5 copy.55
  322.9 1.7 copy.56
  324.6 1.7 copy.57
  (32 shorter events, 8.8 us)
